TPU v7x, 512 devices: a whole 4x8x8 slice. The times are simulated.
512 devices in a mesh: agg: 32 (over x, y_hi, core), sub: 16 (over z, y_lo).
Axes of the slice: x: 4, y: 8 (y_hi: 4, y_lo: 2; y = y_hi * 2 + y_lo), z: 8, core: 2. Of those that a mesh axis runs over, the one named last changes fastest.
Arguments:
- stiffness: float32 [1024, 384, 384], P(('agg', 'sub')), as said below
- face_weight: float32 [1024, 384], P(('agg', 'sub')), may hold values from 0.5 to 4
- face_perm: int32 [1024, 384], P(('agg', 'sub')), may hold values from 0 to 383, each once within a row
- agg_size: int32 [1024], P(('agg', 'sub')), may hold values from 192 to 384
- vec_count: int32 [1024], P(('agg', 'sub')), may hold values from 32 to 64
- start_vecs: float32 [1024, 64, 384], P(('agg', 'sub')), may hold values from -6 to 6
- coarse_map: int32 [1024, 64], P(('agg', 'sub')), may hold values from 0 to 511
- coarse_start: float32 [32, 512, 64], P('agg', 'sub'), may hold values from -6 to 6
Outputs:
- fine_basis: float32 [1024, 64, 384], P(('agg', 'sub'))
- coarse_basis: float32 [32, 512, 64], P('agg', 'sub')
Inputs may be any that keep to these rules, and one draw needn't show every extreme that they name: Each stiffness block is symmetric with a positive diagonal that exceeds the sum of the absolute values of its row's other entries. Each row of face_perm is a permutation of 0 to 383.
All inputs are finite; a program needn't handle non-finite values.
Results may differ from a plain program's by a relative error of at most 0.0003.
Values sent between devices are 32-bit elements; how exact they have to be, the bound alone decides.
A program may use at most 192 MiB of HBM per device.

v0:
```python
import jax
import jax.numpy as jnp
from jax import lax
from jax.sharding import PartitionSpec as P

KC = 512
FSTEPS = 8
CSTEPS = 8


HIGHEST_PRECISION = lax.Precision.HIGHEST


def shifted_2(x, axis, by):
    peers = lax.axis_size(axis)
    return lax.ppermute(x, axis, [(i, (i + by) % peers) for i in range(peers)])


def from_everyone(x, axis):
    peers = lax.axis_size(axis)
    return lax.all_to_all(jnp.broadcast_to(x[None], (peers, *x.shape)), axis, 0, 0, tiled=True)


def joined_along(pieces, dim):
    dims = list(pieces.shape[1:])
    dims[dim] *= pieces.shape[0]
    return jnp.moveaxis(pieces, 0, dim).reshape(dims)


def gathered_copies(x, axis, dim):
    pieces = from_everyone(x, axis)
    return joined_along(pieces, dim)


def fine_level(stiffness, face_sum, agg_size, vec_count, start_vecs):
    fine_order = stiffness.shape[1]
    vec_width = start_vecs.shape[1]
    diagonal = jnp.diagonal(stiffness, axis1=1, axis2=2) + face_sum
    row_totals = jnp.sum(jnp.abs(stiffness), axis=2) + face_sum
    ratio = jnp.max(row_totals / diagonal, axis=1)
    step_scale = 1.0 / (ratio[:, None] * diagonal)
    rows_active = jnp.arange(fine_order, dtype=jnp.int32)[None, :] < agg_size[:, None]
    cols_active = jnp.arange(vec_width, dtype=jnp.int32)[None, :] < vec_count[:, None]
    active = (cols_active[:, :, None] & rows_active[:, None, :]).astype(stiffness.dtype)
    face_rows = face_sum[:, None, :]

    def apply_matrix(vectors):
        product = jnp.einsum("ikn,inm->ikm", vectors, stiffness, precision=HIGHEST_PRECISION)
        return product + vectors * face_rows

    vectors = start_vecs * active
    for sweep in range(FSTEPS):
        vectors = (vectors - step_scale[:, None, :] * apply_matrix(vectors)) * active
    vectors = vectors / jnp.sqrt(jnp.sum(vectors * vectors, axis=2, keepdims=True) + 1e-06)
    applied = apply_matrix(vectors)
    coarse_block = jnp.einsum("ikm,ilm->ikl", vectors, applied, precision=HIGHEST_PRECISION)
    return (vectors, coarse_block)


def assemble(coarse_block, coarse_map):
    selector = (coarse_map[:, :, None] == jnp.arange(KC, dtype=jnp.int32)[None, None, :]).astype(
        coarse_block.dtype
    )
    spread_rows = jnp.einsum("ikl,ilc->ikc", coarse_block, selector, precision=HIGHEST_PRECISION)
    flat_select = selector.reshape(-1, KC)
    flat_spread = spread_rows.reshape(-1, KC)
    return jnp.einsum("kr,kc->rc", flat_select, flat_spread, precision=HIGHEST_PRECISION)


def coarse_whole(partial_value, coarse_start):
    shifted = partial_value + jnp.eye(partial_value.shape[0], dtype=partial_value.dtype)
    diagonal = jnp.diagonal(shifted)
    ratio = jnp.max(jnp.sum(jnp.abs(shifted), axis=1) / diagonal)
    step_scale = 1.0 / (ratio * diagonal)
    iterate = coarse_start
    for sweep in range(CSTEPS):
        iterate = iterate - step_scale[:, None] * jnp.dot(
            shifted, iterate, precision=HIGHEST_PRECISION
        )
    return iterate / jnp.sqrt(jnp.sum(iterate * iterate, axis=0, keepdims=True) + 1e-06)


def local(
    stiffness, face_weight, face_perm, agg_size, vec_count, start_vecs, coarse_map, coarse_start
):
    previous = shifted_2(face_weight, "agg", 1)
    face_sum = face_weight + jnp.take_along_axis(previous, face_perm, axis=1)
    fine_basis, coarse_block = fine_level(stiffness, face_sum, agg_size, vec_count, start_vecs)
    row_count = coarse_start.shape[1]
    offset = lax.axis_index("sub") * row_count
    all_blocks, all_maps = (
        gathered_copies(coarse_block, "sub", 0),
        gathered_copies(coarse_map, "sub", 0),
    )
    assembled = assemble(all_blocks, all_maps)
    start_full = gathered_copies(coarse_start[0], "sub", 0)
    iterate = coarse_whole(assembled, start_full)
    owned = lax.dynamic_slice_in_dim(iterate, offset, row_count, 0)
    return (fine_basis, owned[None])


def solution(mesh):
    placed = (
        P(("agg", "sub"), None, None),
        P(("agg", "sub"), None),
        P(("agg", "sub"), None),
        P(("agg", "sub")),
        P(("agg", "sub")),
        P(("agg", "sub"), None, None),
        P(("agg", "sub"), None),
        P("agg", "sub", None),
    )
    return jax.shard_map(
        local,
        mesh=mesh,
        in_specs=placed,
        out_specs=(P(("agg", "sub"), None, None), P("agg", "sub", None)),
        check_vma=False,
    )
```

profile of v0, /device:TPU:1, one launch (start us, length us, event | category | flops | bytes accessed | tf_op | source)
XLA Modules:
  0.0 139.4 jit_solution(4191286075424917121)
XLA Ops:
  0.6 5.7 %collective-permute-start = (f32[2,384]{1,0:T(2,128)}, f32[2,384]{1,0:T(2,128)S(1)}, u32[]{:S(2)}, u32[]{:S(2)}) collective-permute-start(f32[2,384]{1,0:T(2,128)} %param.9), channel_id=1, source_target_pairs={{0,16},{16,32},{32,48},{48,64},{64,80},{80,96},{96,112},{112,128},... | collective-permute-start | bytes 9224 | tf_op jit(solution)/shard_map/ppermute | solution.py:16
  7.8 11.2 %all-to-all-start.1 = ((s32[16,1,128]{2,1,0:T(1,128)}), s32[16,1,128]{2,1,0:T(1,128)S(1)}, u32[]{:S(2)}, u32[]{:S(2)}) async-start(s32[16,1,128]{2,1,0:T(1,128)} %reshape.113), calls=%async_computation.1 | async-start | bytes 16384 | tf_op jit(solution)/shard_map/all_to_all | solution.py:21
  21.1 1.5 %abs_reduce_fusion = f32[2,384]{1,0:T(2,128)S(1)} fusion(f32[2,384,384]{2,1,0:T(8,128)} %param.8), kind=kLoop, calls=%fused_computation.10 | loop fusion | flops 589056 | bytes 1182720 | tf_op jit(solution)/shard_map/reduce_sum | solution.py:39
  22.5 34.9 %copy.47 = f32[2,384,384]{0,2,1:T(8,128)} copy(f32[2,384,384]{2,1,0:T(8,128)S(1)} %copy-done) | data formatting | bytes 2359296 | tf_op args[0]
  57.5 8.3 %gather_fusion = f32[384,2]{1,0:T(8,128)S(1)} fusion(f32[2,384,384]{0,2,1:T(8,128)} %copy.47, s32[384]{0:T(512)S(1)} %or_reduce_fusion), kind=kCustom, calls=%fused_computation | custom fusion | bytes 9216 | tf_op jit(solution)/shard_map/jit(diagonal)/gather | solution.py:38
  65.9 0.8 reshape.109
  66.8 6.7 %gather_fusion.2 = f32[768]{0:T(1024)S(1)} fusion(f32[2,384]{1,0:T(2,128)S(1)} %collective-permute-done, s32[768]{0:T(1024)S(1)} %reshape.96), kind=kCustom, calls=%fused_computation.2 | custom fusion | bytes 12288 | tf_op jit(solution)/shard_map/jit(take_along_axis)/gather | solution.py:87
  73.7 0.8 fusion.29
  74.6 0.8 fusion.26
  75.4 0.8 fusion.23
  76.2 0.8 fusion.20
  79.5 0.9 multiply_reduce_fusion
  80.5 7.6 %all-to-all-start = ((f32[16,1,2048]{2,1,0:T(1,128)}), f32[16,1,2048]{2,1,0:T(1,128)S(1)}, u32[]{:S(2)}, u32[]{:S(2)}) async-start(f32[16,1,2048]{2,1,0:T(1,128)} %reshape.109), calls=%async_computation | async-start | bytes 262144 | tf_op jit(solution)/shard_map/all_to_all | solution.py:21
  89.4 1.4 %reshape.111 = f32[16,1,8192]{2,1,0:T(1,128)} reshape(f32[16,2,64,64]{3,2,1,0:T(8,128)S(1)} %broadcast_in_dim.24) | data formatting | bytes 1048576
  90.8 5.7 %all-to-all-done = f32[16,1,2048]{2,1,0:T(1,128)S(1)} async-done(((f32[16,1,2048]{2,1,0:T(1,128)}), f32[16,1,2048]{2,1,0:T(1,128)S(1)}, u32[]{:S(2)}, u32[]{:S(2)}) %all-to-all-start) | async-done | bytes 131104 | tf_op jit(solution)/shard_map/all_to_all | solution.py:21
  96.5 3.8 %all-to-all-start.2 = ((f32[16,1,8192]{2,1,0:T(1,128)}), f32[16,1,8192]{2,1,0:T(1,128)S(1)}, u32[]{:S(2)}, u32[]{:S(2)}) async-start(f32[16,1,8192]{2,1,0:T(1,128)} %reshape.111), calls=%async_computation.2 | async-start | bytes 1048576 | tf_op jit(solution)/shard_map/all_to_all | solution.py:21
  102.1 0.9 reduce.2
  103.3 13.7 %all-to-all-done.2 = f32[16,1,8192]{2,1,0:T(1,128)S(1)} async-done(((f32[16,1,8192]{2,1,0:T(1,128)}), f32[16,1,8192]{2,1,0:T(1,128)S(1)}, u32[]{:S(2)}, u32[]{:S(2)}) %all-to-all-start.2) | async-done | bytes 524320 | tf_op jit(solution)/shard_map/all_to_all | solution.py:21
  117.0 1.9 %reduce.3 = f32[16,8192]{1,0:T(8,128)S(1)} reduce(f32[16,1,8192]{2,1,0:T(1,128)S(1)} %all-to-all-done.2, f32[]{:T(128)} %broadcast.136), dimensions={1}, to_apply=%all_to_all.11.reduce_sub_computation | reduce | bytes 1048580 | tf_op jit(solution)/shard_map/all_to_all | solution.py:21
  119.3 2.5 %fusion.1 = f32[32,64,512]{2,1,0:T(8,128)S(1)} fusion(f32[32,64,64]{2,1,0:T(8,128)S(1)} %bitcast.58, s32[32,64]{1,0:T(8,128)S(1)} %bitcast.61), kind=kOutput, calls=%fused_computation.5 | convolution fusion | flops 806354944 | bytes 4726784 | tf_op jit(solution)/shard_map/ikl,ilc->ikc/dot_general | solution.py:64
  121.8 4.3 %abs_reduce_fusion.1 = (f32[512]{0:T(512)S(1)}, f32[512,512]{0,1:T(8,128)S(1)}) fusion(f32[32,64,512]{2,1,0:T(8,128)S(1)} %fusion.1, s32[32,64]{1,0:T(8,128)S(1)} %bitcast.62), kind=kOutput, calls=%fused_computation.60 | convolution fusion | flops 6444809728 | bytes 5253120 | tf_op jit(solution)/shard_map/kr,kc->rc/dot_general | solution.py:67
  126.1 4.8 %gather_fusion.1 = f32[512]{0:T(512)S(1)} fusion(f32[512,512]{0,1:T(8,128)S(1)} %get-tuple-element.7, s32[512]{0:T(512)S(1)} %bitcast.57), kind=kCustom, calls=%fused_computation.1 | custom fusion | bytes 8192 | tf_op jit(solution)/shard_map/jit(diagonal)/cond/branch_0_fun/gather | solution.py:72
  132.1 0.8 fusion.37
  137.7 0.9 multiply_reduce_fusion.1
  (53 shorter events, 16.9 us)
Async XLA Ops:
  0.6 21.9 %copy-start = (f32[2,384,384]{2,1,0:T(8,128)S(1)}, f32[2,384,384]{2,1,0:T(8,128)}, u32[]{:S(2)}) copy-start(f32[2,384,384]{2,1,0:T(8,128)} %param.8) | copy-start | bytes 3538948
  0.6 66.1 %collective-permute-start = (f32[2,384]{1,0:T(2,128)}, f32[2,384]{1,0:T(2,128)S(1)}, u32[]{:S(2)}, u32[]{:S(2)}) collective-permute-start(f32[2,384]{1,0:T(2,128)} %param.9), channel_id=1, source_target_pairs={{0,16},{16,32},{32,48},{48,64},{64,80},{80,96},{96,112},{112,128},... | collective-permute-start | bytes 9224 | tf_op jit(solution)/shard_map/ppermute | solution.py:16
  7.8 72.7 %all-to-all-start.1 = ((s32[16,1,128]{2,1,0:T(1,128)}), s32[16,1,128]{2,1,0:T(1,128)S(1)}, u32[]{:S(2)}, u32[]{:S(2)}) async-start(s32[16,1,128]{2,1,0:T(1,128)} %reshape.113), calls=%async_computation.1 | async-start | bytes 16384 | tf_op jit(solution)/shard_map/all_to_all | solution.py:21
  22.5 43.4 %copy-start.3 = (f32[1,32,64]{2,1,0:T(8,128)S(1)}, f32[1,32,64]{2,1,0:T(8,128)}, u32[]{:S(2)}) copy-start(f32[1,32,64]{2,1,0:T(8,128)} %param.15) | copy-start | bytes 24580
  66.8 6.7 %copy-start.4 = (s32[2,384]{1,0:T(2,128)S(1)}, s32[2,384]{1,0:T(2,128)}, u32[]{:S(2)}) copy-start(s32[2,384]{1,0:T(2,128)} %param.10) | copy-start | bytes 9220
  66.8 6.7 %copy-start.5 = (f32[2,384]{1,0:T(2,128)S(1)}, f32[2,384]{1,0:T(2,128)}, u32[]{:S(2)}) copy-start(f32[2,384]{1,0:T(2,128)} %param.9) | copy-start | bytes 9220
  66.8 6.9 %copy-start.2 = (f32[2,64,384]{2,1,0:T(8,128)S(1)}, f32[2,64,384]{2,1,0:T(8,128)}, u32[]{:S(2)}) copy-start(f32[2,64,384]{2,1,0:T(8,128)} %param.13) | copy-start | bytes 589828
  80.5 8.9 %copy-start.1 = (f32[2,64,384]{2,1,0:T(8,128)}, f32[2,64,384]{2,1,0:T(8,128)S(1)}, u32[]{:S(2)}) copy-start(f32[2,64,384]{2,1,0:T(8,128)S(1)} %broadcast_divide_fusion) | copy-start | bytes 589828
  80.5 16.0 %all-to-all-start = ((f32[16,1,2048]{2,1,0:T(1,128)}), f32[16,1,2048]{2,1,0:T(1,128)S(1)}, u32[]{:S(2)}, u32[]{:S(2)}) async-start(f32[16,1,2048]{2,1,0:T(1,128)} %reshape.109), calls=%async_computation | async-start | bytes 262144 | tf_op jit(solution)/shard_map/all_to_all | solution.py:21
  96.5 20.4 %all-to-all-start.2 = ((f32[16,1,8192]{2,1,0:T(1,128)}), f32[16,1,8192]{2,1,0:T(1,128)S(1)}, u32[]{:S(2)}, u32[]{:S(2)}) async-start(f32[16,1,8192]{2,1,0:T(1,128)} %reshape.111), calls=%async_computation.2 | async-start | bytes 1048576 | tf_op jit(solution)/shard_map/all_to_all | solution.py:21
where the time goes:
time: 140 us; the launch traced here: 139 us
  local copies, waits for them, and re-layouts  61 us (44%)
  starting transfers between devices  28.2 us (20%)
  matrix products  21 us (15%)
  waiting for transfers between devices  19.4 us (14%)
  other arithmetic  8.85 us (6%)
    unnamed x19, local copies, waits for them, and re-layouts  38.5 us
    all_to_all x3, starting transfers between devices, from_everyone(): lax.all_to_all(jnp.broadcast_to(x[None], (peers, *x.shape)), axis, 0, 0,...  22.5 us
    all_to_all x3, waiting for transfers between devices, from_everyone(): lax.all_to_all(jnp.broadcast_to(x[None], (peers, *x.shape)), axis, 0, 0,...  19.4 us
    gather x2, local copies, waits for them, and re-layouts, fine_level(): diagonal = jnp.diagonal(stiffness, axis1=1, axis2=2) + face_sum  8.36 us
    dot_general x9, matrix products, apply_matrix(): jnp.einsum('ikn,inm->ikm', vectors, stiffness, precision=HIGHEST_PRECISION)  7.39 us
    gather x3, local copies, waits for them, and re-layouts, local(): face_sum = face_weight + jnp.take_along_axis(previous, face_perm, axis=1)  6.7 us
    dot_general x8, matrix products, coarse_whole(): jnp.dot(shifted, iterate, precision=HIGHEST_PRECISION)  6.48 us
    ppermute x1, starting transfers between devices, shifted_2(): return lax.ppermute(x, axis, [(i, (i + by) % peers) for i in range(peers)])  5.74 us
  transfers between devices with their start and end apart: 4, of which 2 were waited for; matrix products, arithmetic and copies ran while one was open for 49% of the time, Pallas kernels for 0%

commit v1 on v0

v1 whole, which is shorter than its diff:
```python
import jax
import jax.numpy as jnp
from jax import lax
from jax.experimental import pallas as pl
from jax.experimental.pallas import tpu as pltpu
from jax.sharding import PartitionSpec as P

FSTEPS = 8
CSTEPS = 8
F32 = jnp.float32
BF16 = jnp.bfloat16
LANES = 128
NT = (((1,), (1,)), ((), ()))


def halves(x):
    high = x.astype(BF16)
    low = (x - high.astype(F32)).astype(BF16)
    return high, low


def mm(a, b):
    return jnp.dot(a, b, preferred_element_type=F32)


def mm_nt(a, b):
    return lax.dot_general(a, b, NT, preferred_element_type=F32)


def permuted(face, perm):
    tiles = face.shape[1] // LANES
    out = []
    for t in range(tiles):
        index = perm[:, t * LANES : (t + 1) * LANES]
        low, high = index & (LANES - 1), index >> 7
        total = jnp.zeros(index.shape, F32)
        for s in range(tiles):
            picked = jnp.take_along_axis(face[:, s * LANES : (s + 1) * LANES], low, axis=1)
            total = jnp.where(high == s, picked, total)
        out.append(total)
    return jnp.concatenate(out, axis=1)


def diagonal_parts(load, n):
    eye = lax.broadcasted_iota(jnp.int32, (LANES, LANES), 0) == lax.broadcasted_iota(
        jnp.int32, (LANES, LANES), 1
    )
    diags, sums = [], []
    for c in range(n // LANES):
        total = jnp.zeros((8, LANES), F32)
        for r in range(n // LANES):
            tile = load(r, c)
            if r == c:
                diags.append(jnp.sum(jnp.where(eye, tile, 0.0), axis=0, keepdims=True))
                tile = jnp.where(eye, 0.0, tile)
            yield r, c, tile
            total = total + jnp.sum(jnp.abs(tile).reshape(LANES // 8, 8, LANES), axis=0)
        sums.append(jnp.sum(total, axis=0, keepdims=True))
    yield None, jnp.concatenate(diags, axis=1), jnp.concatenate(sums, axis=1)


def split_matrix(load, store, n):
    for item in diagonal_parts(load, n):
        if item[0] is None:
            return item[1], item[2]
        r, c, tile = item
        high, low = halves(tile)
        store(r, c, high, low)


def product(rows, weights):
    high, low = halves(rows)
    top = jnp.concatenate([high, high], axis=1)
    bottom = jnp.concatenate([low, low], axis=1)
    both = mm(jnp.concatenate([top, bottom], axis=0), weights)
    n = rows.shape[0]
    return both[:n] + both[n:]


def make_kernel(n_agg, n_sub, order, width, kc, kc2):
    n_z = n_sub // 2
    rows_own = kc // n_sub

    def kernel(
        stiff, face_w, perm, asize, vcount, start_vecs, cmap, cstart,
        fine_out, coarse_out,
        s_buf, w_buf, v_buf, face_in, meta_tx, meta_rx, blk_tx, blk_rx,
        sel, spread, assembled, aw, x_all, x_tmp,
        load_sem, out_sem, face_sem, meta_send, meta_recv, blk_send, blk_recv,
    ):
        agg, sub = lax.axis_index("agg"), lax.axis_index("sub")
        nxt, prv = lax.rem(agg + 1, n_agg), lax.rem(agg + n_agg - 1, n_agg)
        z, y = sub // 2, lax.rem(sub, 2)

        def peer(r):
            return lax.rem(z + r // 2, n_z) * 2 + lax.rem(y + r % 2, 2)

        def source(r):
            return lax.rem(z + n_z - r // 2, n_z) * 2 + lax.rem(y + r % 2, 2)

        barrier = pltpu.get_barrier_semaphore()
        for other in (nxt, prv):
            pl.semaphore_signal(barrier, inc=1, device_id={"agg": other})
        for r in range(1, n_sub):
            pl.semaphore_signal(barrier, inc=1, device_id={"sub": peer(r)})

        loads = [pltpu.make_async_copy(stiff.at[i], s_buf.at[i], load_sem.at[i]) for i in range(2)]
        loads.append(pltpu.make_async_copy(start_vecs, v_buf, load_sem.at[2]))
        for load in loads:
            load.start()

        own = cstart[0]
        maps = cmap[...].astype(F32)
        meta_tx[0 : rows_own // 2, 0:kc2] = own[: rows_own // 2]
        meta_tx[0 : rows_own // 2, kc2 : 2 * kc2] = own[rows_own // 2 :]
        meta_tx[rows_own // 2 :, :] = jnp.broadcast_to(
            jnp.concatenate([maps[0:1], maps[1:2]], axis=1), (8, LANES)
        )

        pl.semaphore_wait(barrier, n_sub + 1)

        face_copy = pltpu.make_async_remote_copy(
            face_w, face_in, face_sem.at[0], face_sem.at[1], device_id={"agg": nxt}
        )
        face_copy.start()
        metas = []
        for r in range(1, n_sub):
            metas.append(
                pltpu.make_async_remote_copy(
                    meta_tx, meta_rx.at[r], meta_send.at[r], meta_recv.at[r], device_id={"sub": peer(r)}
                )
            )
            metas[-1].start()

        parts = []
        for i in range(2):
            loads[i].wait()

            def load_tile(r, c, i=i):
                return s_buf[i, r * LANES : (r + 1) * LANES, c * LANES : (c + 1) * LANES]

            def store_tile(r, c, high, low, i=i):
                w_buf[i, r * LANES : (r + 1) * LANES, c * LANES : (c + 1) * LANES] = high
                w_buf[i, order + r * LANES : order + (r + 1) * LANES, c * LANES : (c + 1) * LANES] = low

            parts.append(split_matrix(load_tile, store_tile, order))

        loads[2].wait()
        face_copy.wait()
        faces = face_w[...] + permuted(face_in[...], perm[...])

        lane = lax.broadcasted_iota(jnp.int32, (1, order), 1)
        row = lax.broadcasted_iota(jnp.int32, (width, 1), 0)
        vecs, scales, keeps, diags = [], [], [], []
        for i in range(2):
            diag = parts[i][0] + faces[i : i + 1]
            ratio = jnp.max((parts[i][1] + diag) / diag, axis=1, keepdims=True)
            live = lane < asize[i]
            vecs.append(jnp.where((row < vcount[i]) & live, v_buf[i], 0.0))
            scales.append(jnp.where(live, 1.0 / (ratio * diag), 0.0))
            keeps.append(1.0 - 1.0 / ratio)
            diags.append(diag)
        for _ in range(FSTEPS):
            for i in range(2):
                vecs[i] = vecs[i] * keeps[i] - scales[i] * product(vecs[i], w_buf[i])
        mixed = []
        for i in range(2):
            applied = product(vecs[i], w_buf[i]) + vecs[i] * diags[i]
            inverse = 1.0 / jnp.sqrt(jnp.sum(vecs[i] * vecs[i], axis=1, keepdims=True) + 1e-06)
            basis = vecs[i] * inverse
            v_buf[i] = basis
            ah, al = halves(applied * inverse)
            bh, bl = halves(basis)
            quads = mm_nt(jnp.concatenate([ah, al], axis=0), jnp.concatenate([bh, bl], axis=0))
            pair = quads[:width] + quads[width:]
            mixed.append(pair + pltpu.roll(pair, width, 1))
        left = lax.broadcasted_iota(jnp.int32, (width, LANES), 1) < width
        blk_tx[...] = jnp.where(left, mixed[0], mixed[1])
        fine_copy = pltpu.make_async_copy(v_buf, fine_out, out_sem)
        fine_copy.start()

        blocks = []
        for r in range(1, n_sub):
            blocks.append(
                pltpu.make_async_remote_copy(
                    blk_tx, blk_rx.at[r], blk_send.at[r], blk_recv.at[r], device_id={"sub": peer(r)}
                )
            )
            blocks[-1].start()

        coarse_row = lax.broadcasted_iota(jnp.int32, (kc, LANES), 0).astype(F32)
        for r in range(n_sub):
            if r:
                metas[r - 1].wait()
            got = meta_rx[r] if r else meta_tx[...]
            at = pl.multiple_of(source(r) * rows_own, rows_own)
            x_all[pl.ds(at, rows_own // 2), :] = got[: rows_own // 2]
            x_all[pl.ds(at + rows_own // 2, rows_own // 2), :] = pltpu.roll(
                got[: rows_own // 2], kc2, 1
            )
            sel[:, r * LANES : (r + 1) * LANES] = jnp.where(
                coarse_row == got[rows_own // 2 : rows_own // 2 + 1], 1.0, 0.0
            ).astype(BF16)
        x = x_all[:, 0:kc2].T

        batches = [range(0, 4), range(4, 8), range(8, 12), range(12, 16)]
        for b, batch in enumerate(batches):
            for r in batch:
                if r:
                    blocks[r - 1].wait()
                got = blk_rx[r] if r else blk_tx[...]
                square = jnp.concatenate(
                    [jnp.where(left, got, 0.0), jnp.where(left, 0.0, got)], axis=0
                )
                high, low = halves(square)
                one = sel[:, r * LANES : (r + 1) * LANES]
                wide = mm(one, jnp.concatenate([high, low], axis=1))
                high, low = halves(wide[:, :LANES] + wide[:, LANES:])
                spread[0, :, r * LANES : (r + 1) * LANES] = high
                spread[1, :, r * LANES : (r + 1) * LANES] = low
            span = slice(batch[0] * LANES, (batch[-1] + 1) * LANES)
            gain = mm_nt(spread[0, :, span], sel[:, span]) + mm_nt(spread[1, :, span], sel[:, span])
            assembled[...] = gain if b == 0 else assembled[...] + gain

        def load_tile(r, c):
            return assembled[r * LANES : (r + 1) * LANES, c * LANES : (c + 1) * LANES]

        def store_tile(r, c, high, low):
            aw[r * LANES : (r + 1) * LANES, c * LANES : (c + 1) * LANES] = high
            aw[kc + r * LANES : kc + (r + 1) * LANES, c * LANES : (c + 1) * LANES] = low

        cdiag, csum = split_matrix(load_tile, store_tile, kc)
        cdiag = cdiag + 1.0
        ratio = jnp.max((csum + jnp.abs(cdiag)) / cdiag, axis=1, keepdims=True)
        scale = 1.0 / (ratio * cdiag)
        keep = 1.0 - 1.0 / ratio
        for _ in range(CSTEPS):
            x = x * keep - scale * product(x, aw[...])
        x = x / jnp.sqrt(jnp.sum(x * x, axis=1, keepdims=True) + 1e-06)
        for t in range(kc // LANES):
            x_tmp[t] = x[:, t * LANES : (t + 1) * LANES]
        per = LANES // rows_own
        x_all[0:LANES, 0:kc2] = x_tmp[sub // per].T
        coarse_out[0] = x_all[pl.ds(pl.multiple_of(lax.rem(sub, per) * rows_own, rows_own), rows_own), 0:kc2]

        fine_copy.wait()

    return kernel


def local(stiffness, face_weight, face_perm, agg_size, vec_count, start_vecs, coarse_map, coarse_start, n_agg, n_sub):
    order, width = stiffness.shape[1], start_vecs.shape[1]
    rows_own, kc2 = coarse_start.shape[1:]
    kc = rows_own * n_sub
    vmem = pl.BlockSpec(memory_space=pltpu.VMEM)
    smem = pl.BlockSpec(memory_space=pltpu.SMEM)
    hbm = pl.BlockSpec(memory_space=pl.ANY)
    dma = pltpu.SemaphoreType.DMA
    return pl.pallas_call(
        make_kernel(n_agg, n_sub, order, width, kc, kc2),
        out_shape=(
            jax.ShapeDtypeStruct(start_vecs.shape, F32),
            jax.ShapeDtypeStruct(coarse_start.shape, F32),
        ),
        in_specs=[hbm, vmem, vmem, smem, smem, hbm, vmem, vmem],
        out_specs=(hbm, vmem),
        scratch_shapes=[
            pltpu.VMEM((2, order, order), F32),
            pltpu.VMEM((2, 2 * order, order), BF16),
            pltpu.VMEM((2, width, order), F32),
            pltpu.VMEM((2, order), F32),
            pltpu.VMEM((rows_own // 2 + 8, LANES), F32),
            pltpu.VMEM((n_sub, rows_own // 2 + 8, LANES), F32),
            pltpu.VMEM((width, LANES), F32),
            pltpu.VMEM((n_sub, width, LANES), F32),
            pltpu.VMEM((kc, n_sub * LANES), BF16),
            pltpu.VMEM((2, kc, n_sub * LANES), BF16),
            pltpu.VMEM((kc, kc), F32),
            pltpu.VMEM((2 * kc, kc), BF16),
            pltpu.VMEM((kc, LANES), F32),
            pltpu.VMEM((kc // LANES, kc2, LANES), F32),
            dma((3,)), dma, dma((2,)), dma((n_sub,)), dma((n_sub,)), dma((n_sub,)), dma((n_sub,)),
        ],
        compiler_params=pltpu.CompilerParams(
            collective_id=0, has_side_effects=True, vmem_limit_bytes=40 * 1024 * 1024
        ),
    )(stiffness, face_weight, face_perm, agg_size, vec_count, start_vecs, coarse_map, coarse_start)


def solution(mesh):
    n_agg, n_sub = mesh.shape["agg"], mesh.shape["sub"]
    placed = (
        P(("agg", "sub"), None, None),
        P(("agg", "sub"), None),
        P(("agg", "sub"), None),
        P(("agg", "sub")),
        P(("agg", "sub")),
        P(("agg", "sub"), None, None),
        P(("agg", "sub"), None),
        P("agg", "sub", None),
    )

    def run(*args):
        return local(*args, n_agg, n_sub)

    return jax.shard_map(
        run,
        mesh=mesh,
        in_specs=placed,
        out_specs=(P(("agg", "sub"), None, None), P("agg", "sub", None)),
        check_vma=False,
    )
```

time: 140 us -> 46.7 us (0.33)
  the two profiles are of different devices: /device:TPU:1 before, /device:TPU:8 now
where the time goes in v1:
time: 46.7 us; the launch traced here: 46.4 us
  Pallas kernels  38.2 us (82%)
  local copies, waits for them, and re-layouts  7.55 us (16%)
  between operations  0.66 us (1%)
    pallas_call x1, Pallas kernels, local(): pl.pallas_call(make_kernel(n_agg, n_sub, order, width, kc, kc2), out_shap...  38.2 us
    unnamed x18, local copies, waits for them, and re-layouts  7.55 us

profile of v1, /device:TPU:8, one launch (start us, length us, event | category | flops | bytes accessed | tf_op | source)
XLA Modules:
  0.0 46.4 jit_solution(7655160454234670834)
XLA Ops:
  0.6 0.0 copy-start
  0.6 1.3 %copy-done = f32[2,384,384]{2,1,0:T(8,128)S(1)} copy-done((f32[2,384,384]{2,1,0:T(8,128)S(1)}, f32[2,384,384]{2,1,0:T(8,128)}, u32[]{:S(2)}) %copy-start) | copy-done | bytes 1179672
  1.9 0.0 copy-start.1
  1.9 0.9 %copy-done.1 = f32[2,64,384]{2,1,0:T(8,128)S(1)} copy-done((f32[2,64,384]{2,1,0:T(8,128)S(1)}, f32[2,64,384]{2,1,0:T(8,128)}, u32[]{:S(2)}) %copy-start.1) | copy-done | bytes 196632
  2.8 0.0 copy-start.2
  2.8 0.7 %copy-done.2 = f32[1,32,64]{2,1,0:T(8,128)S(1)} copy-done((f32[1,32,64]{2,1,0:T(8,128)S(1)}, f32[1,32,64]{2,1,0:T(8,128)}, u32[]{:S(2)}) %copy-start.2) | copy-done | bytes 8216
  3.5 0.0 copy-start.3
  3.6 0.7 %copy-done.3 = f32[2,384]{1,0:T(2,128)S(1)} copy-done((f32[2,384]{1,0:T(2,128)S(1)}, f32[2,384]{1,0:T(2,128)}, u32[]{:S(2)}) %copy-start.3) | copy-done | bytes 3096
  4.2 0.0 copy-start.4
  4.2 0.7 %copy-done.4 = s32[2,384]{1,0:T(2,128)S(1)} copy-done((s32[2,384]{1,0:T(2,128)S(1)}, s32[2,384]{1,0:T(2,128)}, u32[]{:S(2)}) %copy-start.4) | copy-done | bytes 3096
  4.9 0.0 copy-start.5
  4.9 0.7 %copy-done.5 = s32[2,64]{1,0:T(2,128)S(1)} copy-done((s32[2,64]{1,0:T(2,128)S(1)}, s32[2,64]{1,0:T(2,128)}, u32[]{:S(2)}) %copy-start.5) | copy-done | bytes 536
  5.6 0.0 copy-start.6
  5.6 0.7 %copy-done.6 = s32[2]{0:T(128)S(1)} copy-done((s32[2]{0:T(128)S(1)}, s32[2]{0:T(128)}, u32[]{:S(2)}) %copy-start.6) | copy-done | bytes 32
  6.3 0.0 copy-start.7
  6.3 0.7 %copy-done.7 = s32[2]{0:T(128)S(1)} copy-done((s32[2]{0:T(128)S(1)}, s32[2]{0:T(128)}, u32[]{:S(2)}) %copy-start.7) | copy-done | bytes 32
  6.9 38.2 %shard_map.95 = (f32[2,64,384]{2,1,0:T(8,128)S(1)}, f32[1,32,64]{2,1,0:T(8,128)S(1)}) custom-call(f32[2,384,384]{2,1,0:T(8,128)S(1)} %copy-done, f32[2,384]{1,0:T(2,128)S(1)} %copy-done.3, s32[2,384]{1,0:T(2,128)S(1)} %copy-done.4, s32[2]{0:T(128)S(1)} %copy-done.6, s32[2]{0:T(128)S(1)} %copy-done.7, f32[2,64,384]{2,1,0:T(8,128)S(1)} %copy-done.1, ...), custom_call_target="tpu_custom_call" | custom-call | tf_op jit(solution)/shard_map/pallas_call | solution.py:259
  45.1 0.7 %copy.12 = f32[2,64,384]{2,1,0:T(8,128)} copy(f32[2,64,384]{2,1,0:T(8,128)S(1)} %get-tuple-element.4) | data formatting | bytes 393216
  45.8 0.6 %copy.13 = f32[1,32,64]{2,1,0:T(8,128)} copy(f32[1,32,64]{2,1,0:T(8,128)S(1)} %get-tuple-element.5) | data formatting | bytes 16384
Async XLA Ops:
  0.6 1.3 %copy-start = (f32[2,384,384]{2,1,0:T(8,128)S(1)}, f32[2,384,384]{2,1,0:T(8,128)}, u32[]{:S(2)}) copy-start(f32[2,384,384]{2,1,0:T(8,128)} %stiff.1) | copy-start | bytes 3538948
  1.9 0.9 %copy-start.1 = (f32[2,64,384]{2,1,0:T(8,128)S(1)}, f32[2,64,384]{2,1,0:T(8,128)}, u32[]{:S(2)}) copy-start(f32[2,64,384]{2,1,0:T(8,128)} %start_vecs.1) | copy-start | bytes 589828
  2.8 0.7 %copy-start.2 = (f32[1,32,64]{2,1,0:T(8,128)S(1)}, f32[1,32,64]{2,1,0:T(8,128)}, u32[]{:S(2)}) copy-start(f32[1,32,64]{2,1,0:T(8,128)} %cstart.1) | copy-start | bytes 24580
  3.5 0.7 %copy-start.3 = (f32[2,384]{1,0:T(2,128)S(1)}, f32[2,384]{1,0:T(2,128)}, u32[]{:S(2)}) copy-start(f32[2,384]{1,0:T(2,128)} %face_w.1) | copy-start | bytes 9220
  4.2 0.7 %copy-start.4 = (s32[2,384]{1,0:T(2,128)S(1)}, s32[2,384]{1,0:T(2,128)}, u32[]{:S(2)}) copy-start(s32[2,384]{1,0:T(2,128)} %perm.1) | copy-start | bytes 9220
  4.9 0.7 %copy-start.5 = (s32[2,64]{1,0:T(2,128)S(1)}, s32[2,64]{1,0:T(2,128)}, u32[]{:S(2)}) copy-start(s32[2,64]{1,0:T(2,128)} %cmap.1) | copy-start | bytes 1540
  5.6 0.7 %copy-start.6 = (s32[2]{0:T(128)S(1)}, s32[2]{0:T(128)}, u32[]{:S(2)}) copy-start(s32[2]{0:T(128)} %asize.1) | copy-start | bytes 28
  6.3 0.7 %copy-start.7 = (s32[2]{0:T(128)S(1)}, s32[2]{0:T(128)}, u32[]{:S(2)}) copy-start(s32[2]{0:T(128)} %vcount.1) | copy-start | bytes 28

commit v2 on v1

--- a/solution.py
+++ b/solution.py
@@ -7,6 +7,7 @@
 
 FSTEPS = 8
 CSTEPS = 8
+BATCHES = ((0,), (1, 2, 14), (3, 15, 4, 12), (5, 13, 6, 10), (7, 11, 8, 9))
 F32 = jnp.float32
 BF16 = jnp.bfloat16
 LANES = 128
@@ -79,14 +80,16 @@
 
 def make_kernel(n_agg, n_sub, order, width, kc, kc2):
     n_z = n_sub // 2
+    order_r = sorted(range(1, n_sub), key=lambda r: (min(r // 2, n_z - r // 2), (r % 2)))
     rows_own = kc // n_sub
 
     def kernel(
-        stiff, face_w, perm, asize, vcount, start_vecs, cmap, cstart,
-        fine_out, coarse_out,
-        s_buf, w_buf, v_buf, face_in, meta_tx, meta_rx, blk_tx, blk_rx,
-        sel, spread, assembled, aw, x_all, x_tmp,
-        load_sem, out_sem, face_sem, meta_send, meta_recv, blk_send, blk_recv,
+        stiff, face_hbm, perm_hbm, asize_hbm, vcount_hbm, start_vecs, cmap_hbm, cstart_hbm,
+        v_buf, assembled, x_out,
+        face_w, perm, asize, vcount, cmap, cstart,
+        s_buf, w_buf, face_in, meta_tx, meta_rx, blk_tx, blk_rx,
+        sel, spread, picked, x_all,
+        load_sem, face_sem, meta_send, meta_recv, blk_send, blk_recv,
     ):
         agg, sub = lax.axis_index("agg"), lax.axis_index("sub")
         nxt, prv = lax.rem(agg + 1, n_agg), lax.rem(agg + n_agg - 1, n_agg)
@@ -101,20 +104,35 @@
         barrier = pltpu.get_barrier_semaphore()
         for other in (nxt, prv):
             pl.semaphore_signal(barrier, inc=1, device_id={"agg": other})
-        for r in range(1, n_sub):
+        for r in order_r:
             pl.semaphore_signal(barrier, inc=1, device_id={"sub": peer(r)})
 
-        loads = [pltpu.make_async_copy(stiff.at[i], s_buf.at[i], load_sem.at[i]) for i in range(2)]
-        loads.append(pltpu.make_async_copy(start_vecs, v_buf, load_sem.at[2]))
+        def to_everyone(mine, slots, send_sem, recv_sem):
+            copies = {}
+            for r in order_r:
+                copies[r] = pltpu.make_async_remote_copy(
+                    mine, slots.at[r], send_sem.at[r], recv_sem.at[r], device_id={"sub": peer(r)}
+                )
+                copies[r].start()
+            return copies
+
+        pairs = [
+            (face_hbm, face_w), (cstart_hbm, cstart), (cmap_hbm, cmap),
+            (stiff.at[0], s_buf.at[0]), (stiff.at[1], s_buf.at[1]), (perm_hbm, perm),
+            (asize_hbm, asize), (vcount_hbm, vcount), (start_vecs, v_buf),
+        ]
+        loads = [pltpu.make_async_copy(a, b, load_sem.at[i]) for i, (a, b) in enumerate(pairs)]
         for load in loads:
             load.start()
+        for load in loads[:3]:
+            load.wait()
 
         own = cstart[0]
         maps = cmap[...].astype(F32)
         meta_tx[0 : rows_own // 2, 0:kc2] = own[: rows_own // 2]
         meta_tx[0 : rows_own // 2, kc2 : 2 * kc2] = own[rows_own // 2 :]
         meta_tx[rows_own // 2 :, :] = jnp.broadcast_to(
-            jnp.concatenate([maps[0:1], maps[1:2]], axis=1), (8, LANES)
+            jnp.concatenate([maps[0:1], maps[1:2]], axis=1), (1, LANES)
         )
 
         pl.semaphore_wait(barrier, n_sub + 1)
@@ -123,18 +141,11 @@
             face_w, face_in, face_sem.at[0], face_sem.at[1], device_id={"agg": nxt}
         )
         face_copy.start()
-        metas = []
-        for r in range(1, n_sub):
-            metas.append(
-                pltpu.make_async_remote_copy(
-                    meta_tx, meta_rx.at[r], meta_send.at[r], meta_recv.at[r], device_id={"sub": peer(r)}
-                )
-            )
-            metas[-1].start()
+        metas = to_everyone(meta_tx, meta_rx, meta_send, meta_recv)
 
         parts = []
         for i in range(2):
-            loads[i].wait()
+            loads[3 + i].wait()
 
             def load_tile(r, c, i=i):
                 return s_buf[i, r * LANES : (r + 1) * LANES, c * LANES : (c + 1) * LANES]
@@ -145,7 +156,8 @@
 
             parts.append(split_matrix(load_tile, store_tile, order))
 
-        loads[2].wait()
+        for load in loads[5:]:
+            load.wait()
         face_copy.wait()
         faces = face_w[...] + permuted(face_in[...], perm[...])
 
@@ -160,7 +172,7 @@
             scales.append(jnp.where(live, 1.0 / (ratio * diag), 0.0))
             keeps.append(1.0 - 1.0 / ratio)
             diags.append(diag)
-        for _ in range(FSTEPS):
+        for sweep in range(FSTEPS):
             for i in range(2):
                 vecs[i] = vecs[i] * keeps[i] - scales[i] * product(vecs[i], w_buf[i])
         mixed = []
@@ -174,24 +186,22 @@
             quads = mm_nt(jnp.concatenate([ah, al], axis=0), jnp.concatenate([bh, bl], axis=0))
             pair = quads[:width] + quads[width:]
             mixed.append(pair + pltpu.roll(pair, width, 1))
-        left = lax.broadcasted_iota(jnp.int32, (width, LANES), 1) < width
-        blk_tx[...] = jnp.where(left, mixed[0], mixed[1])
-        fine_copy = pltpu.make_async_copy(v_buf, fine_out, out_sem)
-        fine_copy.start()
-
-        blocks = []
-        for r in range(1, n_sub):
-            blocks.append(
-                pltpu.make_async_remote_copy(
-                    blk_tx, blk_rx.at[r], blk_send.at[r], blk_recv.at[r], device_id={"sub": peer(r)}
-                )
-            )
-            blocks[-1].start()
+        half = width // 2
+        k = lax.broadcasted_iota(jnp.int32, (half, LANES), 0)
+        lane = lax.broadcasted_iota(jnp.int32, (half, LANES), 1)
+        left = lane < width
+        column = jnp.where(left, lane, lane - width)
+        k = jnp.where(left, k, k + half)
+        first, second = [jnp.where(left, m[:half], m[half:]) for m in mixed]
+        blk_tx[0:half, :] = jnp.where(column >= k, first, second)
+        ends = jnp.sum(jnp.where(column == k, second, 0.0), axis=0, keepdims=True)
+        blk_tx[half : half + 1, :] = jnp.where(lane[0:1] < width + half, pltpu.roll(ends, width, 1), ends)
+        blocks = to_everyone(blk_tx, blk_rx, blk_send, blk_recv)
 
         coarse_row = lax.broadcasted_iota(jnp.int32, (kc, LANES), 0).astype(F32)
         for r in range(n_sub):
             if r:
-                metas[r - 1].wait()
+                metas[r].wait()
             got = meta_rx[r] if r else meta_tx[...]
             at = pl.multiple_of(source(r) * rows_own, rows_own)
             x_all[pl.ds(at, rows_own // 2), :] = got[: rows_own // 2]
@@ -201,26 +211,56 @@
             sel[:, r * LANES : (r + 1) * LANES] = jnp.where(
                 coarse_row == got[rows_own // 2 : rows_own // 2 + 1], 1.0, 0.0
             ).astype(BF16)
-        x = x_all[:, 0:kc2].T
-
-        batches = [range(0, 4), range(4, 8), range(8, 12), range(12, 16)]
-        for b, batch in enumerate(batches):
-            for r in batch:
-                if r:
-                    blocks[r - 1].wait()
+        x_out[...] = x_all[:, 0:kc2].T
+
+        rows = lax.broadcasted_iota(jnp.int32, (LANES, LANES), 0)
+        cols = lax.broadcasted_iota(jnp.int32, (LANES, LANES), 1)
+        top, early = rows < width, cols < width
+        as_is = (top & early & (rows <= cols)) | (~top & ~early & (rows > cols))
+        turned = (top & early & (rows > cols)) | (~top & ~early & (rows < cols))
+        ends_at = ~top & (rows == cols)
+
+        def assemble(batch, slot, begin):
+            for n, r in enumerate(batch):
                 got = blk_rx[r] if r else blk_tx[...]
-                square = jnp.concatenate(
-                    [jnp.where(left, got, 0.0), jnp.where(left, 0.0, got)], axis=0
-                )
+                own, rolled = got[:half], pltpu.roll(got[:half], width, 1)
+                upper, lower = jnp.where(left, own, rolled), jnp.where(left, rolled, own)
+                whole = jnp.concatenate([upper, lower, upper, lower], axis=0)
+                square = jnp.where(as_is, whole, jnp.where(turned, whole.T, 0.0))
+                square = jnp.where(ends_at, got[half : half + 1], square)
                 high, low = halves(square)
                 one = sel[:, r * LANES : (r + 1) * LANES]
                 wide = mm(one, jnp.concatenate([high, low], axis=1))
                 high, low = halves(wide[:, :LANES] + wide[:, LANES:])
-                spread[0, :, r * LANES : (r + 1) * LANES] = high
-                spread[1, :, r * LANES : (r + 1) * LANES] = low
-            span = slice(batch[0] * LANES, (batch[-1] + 1) * LANES)
-            gain = mm_nt(spread[0, :, span], sel[:, span]) + mm_nt(spread[1, :, span], sel[:, span])
-            assembled[...] = gain if b == 0 else assembled[...] + gain
+                at = (slot + n) * LANES
+                spread[:, at : at + LANES] = high
+                spread[:, n_sub * LANES + at : n_sub * LANES + at + LANES] = low
+                picked[:, at : at + LANES] = one
+            at, to = slot * LANES, (slot + len(batch)) * LANES
+            past = n_sub * LANES
+            gain = mm_nt(spread[:, at:to], picked[:, at:to]) + mm_nt(
+                spread[:, past + at : past + to], picked[:, at:to]
+            )
+            assembled[...] = gain if begin else assembled[...] + gain
+
+        slot = 0
+        for batch in BATCHES:
+            for r in batch:
+                if r:
+                    blocks[r].wait()
+            assemble(batch, slot, slot == 0)
+            slot += len(batch)
+
+    return kernel
+
+
+def make_coarse(n_sub, kc, kc2):
+    rows_own = kc // n_sub
+
+    def kernel(basis, assembled, x_in, fine_out, coarse_out, aw, x_tmp, x_cols, x_own, out_sem):
+        sub = lax.axis_index("sub")
+        copies = [pltpu.make_async_copy(basis, fine_out, out_sem.at[0])]
+        copies[0].start()
 
         def load_tile(r, c):
             return assembled[r * LANES : (r + 1) * LANES, c * LANES : (c + 1) * LANES]
@@ -234,57 +274,82 @@
         ratio = jnp.max((csum + jnp.abs(cdiag)) / cdiag, axis=1, keepdims=True)
         scale = 1.0 / (ratio * cdiag)
         keep = 1.0 - 1.0 / ratio
+        x = x_in[...]
         for _ in range(CSTEPS):
             x = x * keep - scale * product(x, aw[...])
         x = x / jnp.sqrt(jnp.sum(x * x, axis=1, keepdims=True) + 1e-06)
         for t in range(kc // LANES):
             x_tmp[t] = x[:, t * LANES : (t + 1) * LANES]
         per = LANES // rows_own
-        x_all[0:LANES, 0:kc2] = x_tmp[sub // per].T
-        coarse_out[0] = x_all[pl.ds(pl.multiple_of(lax.rem(sub, per) * rows_own, rows_own), rows_own), 0:kc2]
-
-        fine_copy.wait()
+        x_cols[...] = x_tmp[sub // per].T
+        x_own[0] = x_cols[pl.ds(pl.multiple_of(lax.rem(sub, per) * rows_own, rows_own), rows_own), :]
+        copies.append(pltpu.make_async_copy(x_own, coarse_out, out_sem.at[1]))
+        copies[1].start()
+
+        for copy in copies:
+            copy.wait()
 
     return kernel
 
 
 def local(stiffness, face_weight, face_perm, agg_size, vec_count, start_vecs, coarse_map, coarse_start, n_agg, n_sub):
+    args = (stiffness, face_weight, face_perm, agg_size, vec_count, start_vecs, coarse_map, coarse_start)
     order, width = stiffness.shape[1], start_vecs.shape[1]
     rows_own, kc2 = coarse_start.shape[1:]
     kc = rows_own * n_sub
     vmem = pl.BlockSpec(memory_space=pltpu.VMEM)
-    smem = pl.BlockSpec(memory_space=pltpu.SMEM)
-    hbm = pl.BlockSpec(memory_space=pl.ANY)
+    hbm = pl.BlockSpec(memory_space=pltpu.HBM)
     dma = pltpu.SemaphoreType.DMA
+    basis, assembled, x = pl.pallas_call(
+        make_kernel(n_agg, n_sub, order, width, kc, kc2),
+        out_shape=(
+            jax.ShapeDtypeStruct(start_vecs.shape, F32),
+            jax.ShapeDtypeStruct((kc, kc), F32),
+            jax.ShapeDtypeStruct((kc2, kc), F32),
+        ),
+        in_specs=[hbm] * 8,
+        out_specs=(vmem, vmem, vmem),
+        scratch_shapes=[
+            pltpu.VMEM((2, order), F32),
+            pltpu.VMEM((2, order), jnp.int32),
+            pltpu.SMEM((2,), jnp.int32),
+            pltpu.SMEM((2,), jnp.int32),
+            pltpu.VMEM((2, width), jnp.int32),
+            pltpu.VMEM((1, rows_own, kc2), F32),
+            pltpu.VMEM((2, order, order), F32),
+            pltpu.VMEM((2, 2 * order, order), BF16),
+            pltpu.VMEM((2, order), F32),
+            pltpu.VMEM((rows_own // 2 + 1, LANES), F32),
+            pltpu.VMEM((n_sub, rows_own // 2 + 1, LANES), F32),
+            pltpu.VMEM((width // 2 + 1, LANES), F32),
+            pltpu.VMEM((n_sub, width // 2 + 1, LANES), F32),
+            pltpu.VMEM((kc, n_sub * LANES), BF16),
+            pltpu.VMEM((kc, 2 * n_sub * LANES), BF16),
+            pltpu.VMEM((kc, n_sub * LANES), BF16),
+            pltpu.VMEM((kc, LANES), F32),
+            dma((9,)), dma((2,)), dma((n_sub,)), dma((n_sub,)), dma((n_sub,)), dma((n_sub,)),
+        ],
+        compiler_params=pltpu.CompilerParams(
+            collective_id=0, has_side_effects=True, vmem_limit_bytes=32 * 1024 * 1024
+        ),
+    )(*[pltpu.with_memory_space_constraint(a, pltpu.HBM) for a in args])
     return pl.pallas_call(
-        make_kernel(n_agg, n_sub, order, width, kc, kc2),
+        make_coarse(n_sub, kc, kc2),
         out_shape=(
             jax.ShapeDtypeStruct(start_vecs.shape, F32),
             jax.ShapeDtypeStruct(coarse_start.shape, F32),
         ),
-        in_specs=[hbm, vmem, vmem, smem, smem, hbm, vmem, vmem],
-        out_specs=(hbm, vmem),
+        in_specs=[vmem] * 3,
+        out_specs=(hbm, hbm),
         scratch_shapes=[
-            pltpu.VMEM((2, order, order), F32),
-            pltpu.VMEM((2, 2 * order, order), BF16),
-            pltpu.VMEM((2, width, order), F32),
-            pltpu.VMEM((2, order), F32),
-            pltpu.VMEM((rows_own // 2 + 8, LANES), F32),
-            pltpu.VMEM((n_sub, rows_own // 2 + 8, LANES), F32),
-            pltpu.VMEM((width, LANES), F32),
-            pltpu.VMEM((n_sub, width, LANES), F32),
-            pltpu.VMEM((kc, n_sub * LANES), BF16),
-            pltpu.VMEM((2, kc, n_sub * LANES), BF16),
-            pltpu.VMEM((kc, kc), F32),
             pltpu.VMEM((2 * kc, kc), BF16),
-            pltpu.VMEM((kc, LANES), F32),
             pltpu.VMEM((kc // LANES, kc2, LANES), F32),
-            dma((3,)), dma, dma((2,)), dma((n_sub,)), dma((n_sub,)), dma((n_sub,)), dma((n_sub,)),
+            pltpu.VMEM((LANES, kc2), F32),
+            pltpu.VMEM((1, rows_own, kc2), F32),
+            dma((2,)),
         ],
-        compiler_params=pltpu.CompilerParams(
-            collective_id=0, has_side_effects=True, vmem_limit_bytes=40 * 1024 * 1024
-        ),
-    )(stiffness, face_weight, face_perm, agg_size, vec_count, start_vecs, coarse_map, coarse_start)
+        compiler_params=pltpu.CompilerParams(vmem_limit_bytes=16 * 1024 * 1024),
+    )(basis, assembled, x)
 
 
 def solution(mesh):

time: 46.7 us -> 32.9 us (0.70)
  local copies, waits for them, and re-layouts: 7.55 us -> 0 us
  Pallas kernels: 38.2 us -> 32.1 us
    pallas_call x1, Pallas kernels: 38.2 us -> 28.8 us  [local(): pl.pallas_call(make_kernel(n_agg, n_sub, order, width, kc, kc2), out_shap...]
    unnamed x18 -> x0, local copies, waits for them, and re-layouts: 7.55 us -> none
    pallas_call x0 -> x1, Pallas kernels: none -> 3.29 us  [local(): pl.pallas_call(make_coarse(n_sub, kc, kc2), out_shape=(jax.ShapeDtypeStru...]
where the time goes in v2:
time: 32.9 us; the launch traced here: 32.8 us
  Pallas kernels  32.1 us (98%)
  between operations  0.64 us (2%)
    pallas_call x1, Pallas kernels, local(): pl.pallas_call(make_kernel(n_agg, n_sub, order, width, kc, kc2), out_shap...  28.8 us
    pallas_call x1, Pallas kernels, local(): pl.pallas_call(make_coarse(n_sub, kc, kc2), out_shape=(jax.ShapeDtypeStru...  3.29 us

profile of v2, /device:TPU:8, one launch (start us, length us, event | category | flops | bytes accessed | tf_op | source)
XLA Modules:
  0.0 32.8 jit_solution(5728369167424810110)
XLA Ops:
  0.6 28.8 %shard_map.95 = (f32[2,64,384]{2,1,0:T(8,128)S(1)}, f32[512,512]{1,0:T(8,128)S(1)}, f32[64,512]{1,0:T(8,128)S(1)}) custom-call(f32[2,384,384]{2,1,0:T(8,128)} %stiff.1, f32[2,384]{1,0:T(2,128)} %face_hbm.1, s32[2,384]{1,0:T(2,128)} %perm_hbm.1, s32[2]{0:T(128)} %asize_hbm.1, s32[2]{0:T(128)} %vcount_hbm.1, f32[2,64,384]{2,1,0:T(8,128)} %start_vecs.1, ...), custom_call_target="tpu_custom_call" | custom-call | tf_op jit(solution)/shard_map/pallas_call | solution.py:303
  29.5 3.3 %shard_map.96 = (f32[2,64,384]{2,1,0:T(8,128)}, f32[1,32,64]{2,1,0:T(8,128)}) custom-call(f32[2,64,384]{2,1,0:T(8,128)S(1)} %get-tuple-element.5.basis, f32[512,512]{1,0:T(8,128)S(1)} %get-tuple-element.6.assembled, f32[64,512]{1,0:T(8,128)S(1)} %get-tuple-element.7.x_in), custom_call_target="tpu_custom_call" | custom-call | tf_op jit(solution)/shard_map/pallas_call | solution.py:336

commit v3 on v2

--- a/solution.py
+++ b/solution.py
@@ -76,6 +76,13 @@
     both = mm(jnp.concatenate([top, bottom], axis=0), weights)
     n = rows.shape[0]
     return both[:n] + both[n:]
+
+
+def product3(rows, weights):
+    high, low = halves(rows)
+    n, k = rows.shape
+    both = mm(jnp.concatenate([high, low], axis=0), weights[:k])
+    return both[:n] + both[n:] + mm(high, weights[k:])
 
 
 def make_kernel(n_agg, n_sub, order, width, kc, kc2):
@@ -233,14 +240,12 @@
                 wide = mm(one, jnp.concatenate([high, low], axis=1))
                 high, low = halves(wide[:, :LANES] + wide[:, LANES:])
                 at = (slot + n) * LANES
-                spread[:, at : at + LANES] = high
-                spread[:, n_sub * LANES + at : n_sub * LANES + at + LANES] = low
+                spread[0:kc, at : at + LANES] = high
+                spread[kc : 2 * kc, at : at + LANES] = low
                 picked[:, at : at + LANES] = one
             at, to = slot * LANES, (slot + len(batch)) * LANES
-            past = n_sub * LANES
-            gain = mm_nt(spread[:, at:to], picked[:, at:to]) + mm_nt(
-                spread[:, past + at : past + to], picked[:, at:to]
-            )
+            gain = mm_nt(spread[:, at:to], picked[:, at:to])
+            gain = gain[:kc] + gain[kc:]
             assembled[...] = gain if begin else assembled[...] + gain
 
         slot = 0
@@ -276,7 +281,7 @@
         keep = 1.0 - 1.0 / ratio
         x = x_in[...]
         for _ in range(CSTEPS):
-            x = x * keep - scale * product(x, aw[...])
+            x = x * keep - scale * product3(x, aw)
         x = x / jnp.sqrt(jnp.sum(x * x, axis=1, keepdims=True) + 1e-06)
         for t in range(kc // LANES):
             x_tmp[t] = x[:, t * LANES : (t + 1) * LANES]
@@ -324,7 +329,7 @@
             pltpu.VMEM((width // 2 + 1, LANES), F32),
             pltpu.VMEM((n_sub, width // 2 + 1, LANES), F32),
             pltpu.VMEM((kc, n_sub * LANES), BF16),
-            pltpu.VMEM((kc, 2 * n_sub * LANES), BF16),
+            pltpu.VMEM((2 * kc, n_sub * LANES), BF16),
             pltpu.VMEM((kc, n_sub * LANES), BF16),
             pltpu.VMEM((kc, LANES), F32),
             dma((9,)), dma((2,)), dma((n_sub,)), dma((n_sub,)), dma((n_sub,)), dma((n_sub,)),

time: 32.9 us -> 32.7 us (level)
  no operation moved by 1% of the time
where the time goes in v3:
time: 32.7 us; the launch traced here: 32.5 us
  Pallas kernels  31.9 us (98%)
  between operations  0.64 us (2%)
    pallas_call x1, Pallas kernels, local(): pl.pallas_call(make_kernel(n_agg, n_sub, order, width, kc, kc2), out_shap...  28.8 us
    pallas_call x1, Pallas kernels, local(): pl.pallas_call(make_coarse(n_sub, kc, kc2), out_shape=(jax.ShapeDtypeStru...  3.08 us

profile of v3, /device:TPU:8, one launch (start us, length us, event | category | flops | bytes accessed | tf_op | source)
XLA Modules:
  0.0 32.5 jit_solution(11823748025867412804)
XLA Ops:
  0.6 28.8 %shard_map.95 = (f32[2,64,384]{2,1,0:T(8,128)S(1)}, f32[512,512]{1,0:T(8,128)S(1)}, f32[64,512]{1,0:T(8,128)S(1)}) custom-call(f32[2,384,384]{2,1,0:T(8,128)} %stiff.1, f32[2,384]{1,0:T(2,128)} %face_hbm.1, s32[2,384]{1,0:T(2,128)} %perm_hbm.1, s32[2]{0:T(128)} %asize_hbm.1, s32[2]{0:T(128)} %vcount_hbm.1, f32[2,64,384]{2,1,0:T(8,128)} %start_vecs.1, ...), custom_call_target="tpu_custom_call" | custom-call | tf_op jit(solution)/shard_map/pallas_call | solution.py:308
  29.5 3.1 %shard_map.96 = (f32[2,64,384]{2,1,0:T(8,128)}, f32[1,32,64]{2,1,0:T(8,128)}) custom-call(f32[2,64,384]{2,1,0:T(8,128)S(1)} %get-tuple-element.5.basis, f32[512,512]{1,0:T(8,128)S(1)} %get-tuple-element.6.assembled, f32[64,512]{1,0:T(8,128)S(1)} %get-tuple-element.7.x_in), custom_call_target="tpu_custom_call" | custom-call | tf_op jit(solution)/shard_map/pallas_call | solution.py:341

commit v4 on v3

--- a/solution.py
+++ b/solution.py
@@ -7,7 +7,7 @@
 
 FSTEPS = 8
 CSTEPS = 8
-BATCHES = ((0,), (1, 2, 14), (3, 15, 4, 12), (5, 13, 6, 10), (7, 11, 8, 9))
+BATCHES = ((0,), (1, 2, 14, 3), (15, 4, 12, 5), (13, 6, 10, 7, 11, 8, 9))
 F32 = jnp.float32
 BF16 = jnp.bfloat16
 LANES = 128
@@ -92,10 +92,10 @@
 
     def kernel(
         stiff, face_hbm, perm_hbm, asize_hbm, vcount_hbm, start_vecs, cmap_hbm, cstart_hbm,
-        v_buf, assembled, x_out,
+        v_buf, aw, crow, x_out,
         face_w, perm, asize, vcount, cmap, cstart,
         s_buf, w_buf, face_in, meta_tx, meta_rx, blk_tx, blk_rx,
-        sel, spread, picked, x_all,
+        sel, spread, picked, x_all, assembled,
         load_sem, face_sem, meta_send, meta_recv, blk_send, blk_recv,
     ):
         agg, sub = lax.axis_index("agg"), lax.axis_index("sub")
@@ -109,9 +109,9 @@
             return lax.rem(z + n_z - r // 2, n_z) * 2 + lax.rem(y + r % 2, 2)
 
         barrier = pltpu.get_barrier_semaphore()
-        for other in (nxt, prv):
+        for other in (prv, nxt):
             pl.semaphore_signal(barrier, inc=1, device_id={"agg": other})
-        for r in order_r:
+        for r in order_r[::-1]:
             pl.semaphore_signal(barrier, inc=1, device_id={"sub": peer(r)})
 
         def to_everyone(mine, slots, send_sem, recv_sem):
@@ -237,16 +237,41 @@
                 square = jnp.where(ends_at, got[half : half + 1], square)
                 high, low = halves(square)
                 one = sel[:, r * LANES : (r + 1) * LANES]
-                wide = mm(one, jnp.concatenate([high, low], axis=1))
-                high, low = halves(wide[:, :LANES] + wide[:, LANES:])
+                wide = mm(jnp.concatenate([one, one], axis=1), jnp.concatenate([high, low], axis=0))
+                high, low = halves(wide)
                 at = (slot + n) * LANES
                 spread[0:kc, at : at + LANES] = high
                 spread[kc : 2 * kc, at : at + LANES] = low
                 picked[:, at : at + LANES] = one
             at, to = slot * LANES, (slot + len(batch)) * LANES
-            gain = mm_nt(spread[:, at:to], picked[:, at:to])
-            gain = gain[:kc] + gain[kc:]
-            assembled[...] = gain if begin else assembled[...] + gain
+            def gain(cols):
+                both = mm_nt(spread[:, at:to], picked[cols, at:to])
+                return both[:kc] + both[kc:]
+
+            if slot + len(batch) < n_sub:
+                everything = gain(slice(0, kc))
+                assembled[...] = everything if begin else assembled[...] + everything
+                return
+            part, ready = 2 * LANES, {}
+
+            def load_tile(r, c):
+                place = c * LANES // part
+                if place not in ready:
+                    ready[place] = gain(slice(place * part, (place + 1) * part))
+                from_row, from_col = r * LANES, c * LANES
+                within = from_col - place * part
+                return (
+                    assembled[from_row : from_row + LANES, from_col : from_col + LANES]
+                    + ready[place][from_row : from_row + LANES, within : within + LANES]
+                )
+
+            def store_tile(r, c, high, low):
+                aw[r * LANES : (r + 1) * LANES, c * LANES : (c + 1) * LANES] = high
+                aw[kc + r * LANES : kc + (r + 1) * LANES, c * LANES : (c + 1) * LANES] = low
+
+            cdiag, csum = split_matrix(load_tile, store_tile, kc)
+            crow[0:1, :] = cdiag
+            crow[1:2, :] = csum
 
         slot = 0
         for batch in BATCHES:
@@ -262,19 +287,12 @@
 def make_coarse(n_sub, kc, kc2):
     rows_own = kc // n_sub
 
-    def kernel(basis, assembled, x_in, fine_out, coarse_out, aw, x_tmp, x_cols, x_own, out_sem):
+    def kernel(basis, aw, crow, x_in, fine_out, coarse_out, x_tmp, x_cols, x_own, out_sem):
         sub = lax.axis_index("sub")
         copies = [pltpu.make_async_copy(basis, fine_out, out_sem.at[0])]
         copies[0].start()
 
-        def load_tile(r, c):
-            return assembled[r * LANES : (r + 1) * LANES, c * LANES : (c + 1) * LANES]
-
-        def store_tile(r, c, high, low):
-            aw[r * LANES : (r + 1) * LANES, c * LANES : (c + 1) * LANES] = high
-            aw[kc + r * LANES : kc + (r + 1) * LANES, c * LANES : (c + 1) * LANES] = low
-
-        cdiag, csum = split_matrix(load_tile, store_tile, kc)
+        cdiag, csum = crow[0:1, :], crow[1:2, :]
         cdiag = cdiag + 1.0
         ratio = jnp.max((csum + jnp.abs(cdiag)) / cdiag, axis=1, keepdims=True)
         scale = 1.0 / (ratio * cdiag)
@@ -305,15 +323,16 @@
     vmem = pl.BlockSpec(memory_space=pltpu.VMEM)
     hbm = pl.BlockSpec(memory_space=pltpu.HBM)
     dma = pltpu.SemaphoreType.DMA
-    basis, assembled, x = pl.pallas_call(
+    basis, aw, crow, x = pl.pallas_call(
         make_kernel(n_agg, n_sub, order, width, kc, kc2),
         out_shape=(
             jax.ShapeDtypeStruct(start_vecs.shape, F32),
-            jax.ShapeDtypeStruct((kc, kc), F32),
+            jax.ShapeDtypeStruct((2 * kc, kc), BF16),
+            jax.ShapeDtypeStruct((8, kc), F32),
             jax.ShapeDtypeStruct((kc2, kc), F32),
         ),
         in_specs=[hbm] * 8,
-        out_specs=(vmem, vmem, vmem),
+        out_specs=(vmem,) * 4,
         scratch_shapes=[
             pltpu.VMEM((2, order), F32),
             pltpu.VMEM((2, order), jnp.int32),
@@ -332,6 +351,7 @@
             pltpu.VMEM((2 * kc, n_sub * LANES), BF16),
             pltpu.VMEM((kc, n_sub * LANES), BF16),
             pltpu.VMEM((kc, LANES), F32),
+            pltpu.VMEM((kc, kc), F32),
             dma((9,)), dma((2,)), dma((n_sub,)), dma((n_sub,)), dma((n_sub,)), dma((n_sub,)),
         ],
         compiler_params=pltpu.CompilerParams(
@@ -344,17 +364,16 @@
             jax.ShapeDtypeStruct(start_vecs.shape, F32),
             jax.ShapeDtypeStruct(coarse_start.shape, F32),
         ),
-        in_specs=[vmem] * 3,
+        in_specs=[vmem] * 4,
         out_specs=(hbm, hbm),
         scratch_shapes=[
-            pltpu.VMEM((2 * kc, kc), BF16),
             pltpu.VMEM((kc // LANES, kc2, LANES), F32),
             pltpu.VMEM((LANES, kc2), F32),
             pltpu.VMEM((1, rows_own, kc2), F32),
             dma((2,)),
         ],
         compiler_params=pltpu.CompilerParams(vmem_limit_bytes=16 * 1024 * 1024),
-    )(basis, assembled, x)
+    )(basis, aw, crow, x)
 
 
 def solution(mesh):

time: 32.7 us -> 32.3 us (0.988)
  Pallas kernels: 31.9 us -> 31.5 us
where the time goes in v4:
time: 32.3 us; the launch traced here: 32.2 us
  Pallas kernels  31.5 us (98%)
  between operations  0.64 us (2%)
    pallas_call x1, Pallas kernels, local(): pl.pallas_call(make_kernel(n_agg, n_sub, order, width, kc, kc2), out_shap...  28.7 us
    pallas_call x1, Pallas kernels, local(): pl.pallas_call(make_coarse(n_sub, kc, kc2), out_shape=(jax.ShapeDtypeStru...  2.87 us

profile of v4, /device:TPU:8, one launch (start us, length us, event | category | flops | bytes accessed | tf_op | source)
XLA Modules:
  0.0 32.2 jit_solution(779442424535844878)
XLA Ops:
  0.6 28.7 %shard_map.95 = (f32[2,64,384]{2,1,0:T(8,128)S(1)}, bf16[1024,512]{1,0:T(8,128)(2,1)S(1)}, f32[8,512]{1,0:T(8,128)S(1)}, f32[64,512]{1,0:T(8,128)S(1)}) custom-call(f32[2,384,384]{2,1,0:T(8,128)} %stiff.1, f32[2,384]{1,0:T(2,128)} %face_hbm.1, s32[2,384]{1,0:T(2,128)} %perm_hbm.1, s32[2]{0:T(128)} %asize_hbm.1, s32[2]{0:T(128)} %vcount_hbm.1, ...), custom_call_target="tpu_custom_call" | custom-call | tf_op jit(solution)/shard_map/pallas_call | solution.py:326
  29.3 2.9 %shard_map.96 = (f32[2,64,384]{2,1,0:T(8,128)}, f32[1,32,64]{2,1,0:T(8,128)}) custom-call(f32[2,64,384]{2,1,0:T(8,128)S(1)} %get-tuple-element.6.basis, bf16[1024,512]{1,0:T(8,128)(2,1)S(1)} %get-tuple-element.7.aw, f32[8,512]{1,0:T(8,128)S(1)} %get-tuple-element.8.crow, f32[64,512]{1,0:T(8,128)S(1)} %get-tuple-element.9.x_in), custom_call_target="tpu_custom_call" | custom-call | tf_op jit(solution)/shard_map/pallas_call | solution.py:361

commit v5 on v4

--- a/solution.py
+++ b/solution.py
@@ -181,7 +181,7 @@
             diags.append(diag)
         for sweep in range(FSTEPS):
             for i in range(2):
-                vecs[i] = vecs[i] * keeps[i] - scales[i] * product(vecs[i], w_buf[i])
+                vecs[i] = vecs[i] * keeps[i] - scales[i] * product3(vecs[i], w_buf.at[i])
         mixed = []
         for i in range(2):
             applied = product(vecs[i], w_buf[i]) + vecs[i] * diags[i]

time: 32.3 us -> 32.4 us (level)
  no operation moved by 1% of the time
where the time goes in v5:
time: 32.4 us; the launch traced here: 32.2 us
  Pallas kernels  31.6 us (98%)
  between operations  0.64 us (2%)
    pallas_call x1, Pallas kernels, local(): pl.pallas_call(make_kernel(n_agg, n_sub, order, width, kc, kc2), out_shap...  28.7 us
    pallas_call x1, Pallas kernels, local(): pl.pallas_call(make_coarse(n_sub, kc, kc2), out_shape=(jax.ShapeDtypeStru...  2.86 us

profile of v5, /device:TPU:8, one launch (start us, length us, event | category | flops | bytes accessed | tf_op | source)
XLA Modules:
  0.0 32.2 jit_solution(2212224615590711229)
XLA Ops:
  0.6 28.7 %shard_map.95 = (f32[2,64,384]{2,1,0:T(8,128)S(1)}, bf16[1024,512]{1,0:T(8,128)(2,1)S(1)}, f32[8,512]{1,0:T(8,128)S(1)}, f32[64,512]{1,0:T(8,128)S(1)}) custom-call(f32[2,384,384]{2,1,0:T(8,128)} %stiff.1, f32[2,384]{1,0:T(2,128)} %face_hbm.1, s32[2,384]{1,0:T(2,128)} %perm_hbm.1, s32[2]{0:T(128)} %asize_hbm.1, s32[2]{0:T(128)} %vcount_hbm.1, ...), custom_call_target="tpu_custom_call" | custom-call | tf_op jit(solution)/shard_map/pallas_call | solution.py:326
  29.4 2.9 %shard_map.96 = (f32[2,64,384]{2,1,0:T(8,128)}, f32[1,32,64]{2,1,0:T(8,128)}) custom-call(f32[2,64,384]{2,1,0:T(8,128)S(1)} %get-tuple-element.6.basis, bf16[1024,512]{1,0:T(8,128)(2,1)S(1)} %get-tuple-element.7.aw, f32[8,512]{1,0:T(8,128)S(1)} %get-tuple-element.8.crow, f32[64,512]{1,0:T(8,128)S(1)} %get-tuple-element.9.x_in), custom_call_target="tpu_custom_call" | custom-call | tf_op jit(solution)/shard_map/pallas_call | solution.py:361
